TPU v7x, 128 devices: a whole 4x4x4 slice. The times are simulated.
128 devices in a mesh: grp: 4 (over y), seq: 32 (over x, z, core).
Axes of the slice: x: 4, y: 4, z: 4, core: 2. Of those that a mesh axis runs over, the one named last changes fastest.
Arguments:
- phonemes: bfloat16 [4, 1536, 1024], P('grp', 'seq'), may hold values from -7 to 7
- durations: int32 [4, 1536], P('grp', 'seq'), may hold values from 1 to 673, as said below
- weights: bfloat16 [4, 1024, 1024], replicated, may hold values from -1 to 1
- d_out: bfloat16 [4, 12288, 1024], P('grp', 'seq'), may hold values from -6 to 6
Outputs:
- d_phonemes: bfloat16 [4, 1536, 1024], P('grp', 'seq')
- d_weights: float32 [4, 1024, 1024], P(None, ('grp', 'seq'))
Inputs may be any that keep to these rules, and one draw needn't show every extreme that they name: In each chapter the durations sum to 12288, and the frames of the 48 phonemes at positions k * 48 to (k + 1) * 48 - 1 lie within frames (k - 1) * 384 to (k + 2) * 384 - 1; in every chapter some such block of phonemes reaches into both of these neighbouring frame ranges, and some phoneme lasts the largest duration.
All inputs are finite; a program needn't handle non-finite values.
Results may differ from a plain program's by a relative error of at most 0.018.
Values may be sent and summed in bfloat16 or wider, within the bound.
A program may use at most 128 MiB of HBM per device.

v0:
```python
import math

import jax
import jax.numpy as jnp
from jax import lax
from jax.sharding import PartitionSpec as P

HEADS = 16
WINDOW = 512


def extended_2(cells, sides, width):
    for axis, dim in sides:
        count = lax.axis_size(axis)
        ends = count - 1
        head = lax.slice_in_dim(cells, 0, width, axis=dim)
        tail = lax.slice_in_dim(cells, cells.shape[dim] - width, cells.shape[dim], axis=dim)
        cells = jnp.concatenate(
            [
                lax.ppermute(tail, axis, [(i, (i + 1) % count) for i in range(ends)]),
                cells,
                lax.ppermute(head, axis, [((i + 1) % count, i) for i in range(ends)]),
            ],
            axis=dim,
        )
    return cells


def shifted(value, axis, steps):
    count = lax.axis_size(axis)
    leading, last = (max(0, -steps), min(count, count - steps))
    return lax.ppermute(value, axis, [(source, source + steps) for source in range(leading, last)])


def position_table(first_frame, frame_count, model_width):
    frame_ids = (first_frame + jnp.arange(frame_count, dtype=jnp.int32)).astype(jnp.float32)
    half_width = model_width // 2
    rates = jnp.exp(jnp.arange(half_width, dtype=jnp.float32) * (-math.log(10000.0) / half_width))
    angles = frame_ids[:, None] * rates[None, :]
    return jnp.concatenate([jnp.sin(angles), jnp.cos(angles)], axis=1)


def split_heads(matrix, head_count):
    return matrix.reshape(matrix.shape[0], head_count, matrix.shape[1] // head_count).transpose(
        1, 0, 2
    )


def merge_heads(stacked):
    return stacked.transpose(1, 0, 2).reshape(stacked.shape[1], stacked.shape[0] * stacked.shape[2])


def window_mask(first_query, first_key, query_rows, key_rows, frames_all, window_size):
    query_pos = first_query + jnp.arange(query_rows, dtype=jnp.int32)[:, None]
    key_pos = first_key + jnp.arange(key_rows, dtype=jnp.int32)[None, :]
    offset = key_pos - query_pos
    half_window = window_size // 2
    return (
        (offset >= -half_window) & (offset < half_window) & (key_pos >= 0) & (key_pos < frames_all)
    )


def probabilities(head_q, head_k, allowed):
    score_scale = head_q.shape[1] ** (-0.5)
    scores = jnp.dot(head_q, head_k.T, preferred_element_type=jnp.float32) * score_scale
    scores = jnp.where(allowed, scores, -jnp.inf)
    row_max = jnp.max(scores, axis=1, keepdims=True)
    exp_scores = jnp.exp(scores - row_max)
    return exp_scores / jnp.sum(exp_scores, axis=1, keepdims=True)


def forward_block(query, keyvals, allowed, head_count):
    model_width = query.shape[1]
    heads_q = split_heads(query, head_count)
    heads_k = split_heads(keyvals[:, :model_width], head_count)
    heads_v = split_heads(keyvals[:, model_width:], head_count)

    def forward_one_head(head_item):
        head_q, head_k, head_v = head_item
        attn_probs = probabilities(head_q, head_k, allowed).astype(jnp.bfloat16)
        return jnp.dot(attn_probs, head_v, preferred_element_type=jnp.float32)

    return merge_heads(lax.map(forward_one_head, (heads_q, heads_k, heads_v))).astype(jnp.bfloat16)


def backward_block(query, keyvals, d_attended, allowed, head_count):
    model_width = query.shape[1]
    heads_q = split_heads(query, head_count)
    heads_k = split_heads(keyvals[:, :model_width], head_count)
    heads_v = split_heads(keyvals[:, model_width:], head_count)
    heads_g = split_heads(d_attended, head_count)
    score_scale = heads_q.shape[2] ** (-0.5)

    def backward_one_head(head_item):
        head_q, head_k, head_v, head_g = head_item
        attn_probs = probabilities(head_q, head_k, allowed)
        probs_low = attn_probs.astype(jnp.bfloat16)
        d_probs = jnp.dot(head_g, head_v.T, preferred_element_type=jnp.float32)
        d_values = jnp.dot(probs_low.T, head_g, preferred_element_type=jnp.float32)
        d_scores = attn_probs * (d_probs - jnp.sum(attn_probs * d_probs, axis=1, keepdims=True))
        d_low = (d_scores * score_scale).astype(jnp.bfloat16)
        d_query = jnp.dot(d_low, head_k, preferred_element_type=jnp.float32)
        d_keys = jnp.dot(d_low.T, head_q, preferred_element_type=jnp.float32)
        return (d_query, d_keys, d_values)

    d_query, d_keys, d_values = lax.map(backward_one_head, (heads_q, heads_k, heads_v, heads_g))
    return (
        merge_heads(d_query),
        jnp.concatenate([merge_heads(d_keys), merge_heads(d_values)], axis=1),
    )


def norm_backward(resid, cotan_low):
    row_mean = jnp.mean(resid, axis=1, keepdims=True)
    centered = resid - row_mean
    inv_std = lax.rsqrt(jnp.mean(centered * centered, axis=1, keepdims=True) + 1e-05)
    normed = centered * inv_std
    cotan = cotan_low.astype(jnp.float32)
    return inv_std * (
        cotan
        - jnp.mean(cotan, axis=1, keepdims=True)
        - normed * jnp.mean(cotan * normed, axis=1, keepdims=True)
    )


def on_device(phonemes, durations, weights, d_out):
    local_phon = phonemes[0]
    lengths = durations[0]
    cotangent = d_out[0]
    f_local, model_width = cotangent.shape
    p_local = local_phon.shape[0]
    seq_count = lax.axis_size("seq")
    seq_index = lax.axis_index("seq")
    frames_all = f_local * seq_count
    half_window = WINDOW // 2
    query_rows = min(f_local, WINDOW)
    block_count = f_local // query_rows
    first_frame = seq_index * f_local
    frame_pos = first_frame + jnp.arange(f_local, dtype=jnp.int32)
    w_query, w_key, w_value, w_out = (weights[0], weights[1], weights[2], weights[3])
    all_lengths = lax.all_gather(lengths, "seq", axis=0, tiled=True)
    phon_ends = jnp.cumsum(all_lengths)
    phon_starts = phon_ends - all_lengths
    nearby = extended_2(local_phon, (("seq", 0),), p_local)
    row_begins = lax.dynamic_slice_in_dim(
        jnp.pad(phon_starts, (p_local, p_local)), seq_index * p_local, 3 * p_local, 0
    )
    row_ends = lax.dynamic_slice_in_dim(
        jnp.pad(phon_ends, (p_local, p_local)), seq_index * p_local, 3 * p_local, 0
    )
    onehot_rows = (
        (frame_pos[:, None] >= row_begins[None, :]) & (frame_pos[:, None] < row_ends[None, :])
    ).astype(jnp.bfloat16)
    expanded = jnp.dot(onehot_rows, nearby, preferred_element_type=jnp.float32)
    inputs = (expanded + position_table(first_frame, f_local, model_width)).astype(jnp.bfloat16)
    query = jnp.dot(inputs, w_query, preferred_element_type=jnp.float32).astype(jnp.bfloat16)
    keys_local = jnp.dot(inputs, w_key, preferred_element_type=jnp.float32).astype(jnp.bfloat16)
    values_local = jnp.dot(inputs, w_value, preferred_element_type=jnp.float32).astype(jnp.bfloat16)
    keyvals = jnp.concatenate([keys_local, values_local], axis=1)
    extended = extended_2(keyvals, (("seq", 0),), half_window)

    def forward_one(block_index):
        row_start = block_index * query_rows
        allowed = window_mask(
            first_frame + row_start,
            first_frame + row_start - half_window,
            query_rows,
            query_rows + WINDOW,
            frames_all,
            WINDOW,
        )
        return forward_block(query, extended, allowed, HEADS)

    block_ids = jnp.arange(block_count, dtype=jnp.int32)
    attended = lax.map(forward_one, block_ids).reshape(f_local, model_width)
    resid = inputs.astype(jnp.float32) + jnp.dot(
        attended, w_out, preferred_element_type=jnp.float32
    )
    d_resid = norm_backward(resid, cotangent)
    d_proj = d_resid.astype(jnp.bfloat16)
    d_attended = jnp.dot(d_proj, w_out.T, preferred_element_type=jnp.float32).astype(jnp.bfloat16)

    def backward_one(carried, block_index):
        row_start = block_index * query_rows
        allowed = window_mask(
            first_frame + row_start,
            first_frame + row_start - half_window,
            query_rows,
            query_rows + WINDOW,
            frames_all,
            WINDOW,
        )
        d_query, d_keyvals = backward_block(query, extended, d_attended, allowed, HEADS)
        existing = carried
        carried = existing + d_keyvals
        return (carried, d_query)

    d_extended, d_query = lax.scan(
        backward_one, jnp.zeros((f_local + WINDOW, 2 * model_width), jnp.float32), block_ids
    )
    from_next = shifted(d_extended[:half_window].astype(jnp.bfloat16), "seq", -1).astype(
        jnp.float32
    )
    from_prev = shifted(d_extended[half_window + f_local :].astype(jnp.bfloat16), "seq", 1).astype(
        jnp.float32
    )
    d_keyvals = d_extended[half_window : half_window + f_local]
    d_keyvals = d_keyvals.at[:half_window].add(from_prev).at[f_local - half_window :].add(from_next)
    d_query = d_query.reshape(f_local, model_width).astype(jnp.bfloat16)
    d_keys = d_keyvals[:, :model_width].astype(jnp.bfloat16)
    d_values = d_keyvals[:, model_width:].astype(jnp.bfloat16)
    grad_scale = 1.0 / math.sqrt(lax.axis_size("grp") * frames_all)
    grad_terms = (
        jnp.stack(
            [
                jnp.dot(inputs.T, d_query, preferred_element_type=jnp.float32),
                jnp.dot(inputs.T, d_keys, preferred_element_type=jnp.float32),
                jnp.dot(inputs.T, d_values, preferred_element_type=jnp.float32),
                jnp.dot(attended.T, d_proj, preferred_element_type=jnp.float32),
            ]
        )
        * grad_scale
    )
    d_weights = lax.psum_scatter(grad_terms, ("grp", "seq"), scatter_dimension=1, tiled=True)
    d_inputs = d_resid + jnp.dot(d_query, w_query.T, preferred_element_type=jnp.float32)
    d_inputs = d_inputs + jnp.dot(d_keys, w_key.T, preferred_element_type=jnp.float32)
    d_inputs = d_inputs + jnp.dot(d_values, w_value.T, preferred_element_type=jnp.float32)
    d_low = d_inputs.astype(jnp.bfloat16)
    near_terms = jnp.dot(onehot_rows.T, d_low, preferred_element_type=jnp.float32)
    sums_next = shifted(near_terms[:p_local].astype(jnp.bfloat16), "seq", -1).astype(jnp.float32)
    sums_prev = shifted(near_terms[2 * p_local :].astype(jnp.bfloat16), "seq", 1).astype(
        jnp.float32
    )
    d_phon = near_terms[p_local : 2 * p_local] + sums_next + sums_prev
    return (d_phon.astype(jnp.bfloat16)[None], d_weights)


def solution(mesh):
    return jax.shard_map(
        on_device,
        mesh=mesh,
        in_specs=(P("grp", "seq", None), P("grp", "seq"), P(), P("grp", "seq", None)),
        out_specs=(P("grp", "seq", None), P(None, ("grp", "seq"), None)),
        check_vma=False,
    )
```

profile of v0, /device:TPU:1, one launch (start us, length us, event | category | flops | bytes accessed | tf_op | source)
XLA Modules:
  0.0 1016.2 jit_solution(2627465296537107513)
XLA Ops:
  7.2 3.3 collective-permute-start.1
  10.6 3.5 collective-permute-start
  16.8 14.4 %all-reduce.2 = s32[1536]{0:T(1024)S(1)} all-reduce(s32[1536]{0:T(1024)S(1)} %bitcast_dynamic-update-slice_fusion), channel_id=2, replica_groups=mesh['grp'=4,'seq'=32] {'seq'}, use_global_device_ids=true, to_apply=%add.2 | all-reduce | flops 1536 | bytes 12288 | tf_op jit(solution)/shard_map/all_gather | solution.py:141
  31.9 2.8 multiply_sine_fusion
  35.2 2.9 fusion.94
  38.1 2.6 fusion.91
  42.3 4.8 collective-permute-start.2
  47.0 2.1 collective-permute-start.3
  49.4 3.7 fusion.88
  56.2 2.9 collective-permute-done.2
  59.1 4.4 collective-permute-done.3
  63.5 2.6 pad_maximum_fusion.1
  67.8 3.8 copy.12
  71.6 4.6 copy.15
  76.2 2.5 copy.11
  78.7 4.6 copy.14
  83.4 58.1 %while.45 = (s32[]{:T(128)}, bf16[16,384,64]{1,2,0:T(8,128)(2,1)S(1)}, bf16[16,384,64]{2,1,0:T(8,128)(2,1)}, bf16[16,896,64]{2,1,0:T(8,128)(2,1)}, bf16[16,896,6...) while((s32[]{:T(128)}, ...), condition=%wide.region_5.6_spmd.clone, body=%wide.region_2.5_spmd.clone.sunk | while | flops 92896512 | bytes 4801901 | solution.py:83
  141.4 2.7 fusion.139
  145.7 3.6 fusion.97
  149.3 2.3 copy.16
  152.6 159.1 %while.46 = (s32[]{:T(128)}, bf16[16,384,64]{1,2,0:T(8,128)(2,1)}, f32[16,896,64]{1,2,0:T(8,128)}, f32[16,896,64]{1,2,0:T(8,128)}, bf16[16,384,64]{2,1,0:T(8,128...) while((s32[]{:T(128)}, bf16[16,384,64]{1,2,0:T(8,128)(2,1)}, ...), condition=%wide.region_14.15_spmd.clone, body=%wide.region_10.14_spmd.clone.sunk | while | flops 228457344 | bytes 13267333 | solution.py:106
  158.7 2.0 fusion.184
  168.6 2.0 fusion.184
  178.5 2.0 fusion.184
  188.5 2.0 fusion.184
  198.4 2.0 fusion.184
  208.4 2.0 fusion.184
  218.3 2.0 fusion.184
  228.3 2.0 fusion.184
  238.2 2.0 fusion.184
  248.2 2.0 fusion.184
  258.1 2.0 fusion.184
  268.1 2.0 fusion.184
  278.0 2.0 fusion.184
  287.9 2.0 fusion.184
  297.8 2.0 fusion.184
  307.8 2.0 fusion.184
  311.6 3.7 fusion.50
  315.5 2.2 collective-permute-start.4
  317.7 2.8 collective-permute-start.5
  323.5 5.9 collective-permute-done.4
  329.6 4.3 collective-permute-done.5
  337.2 6.2 maximum_multiply_fusion
  343.4 4.1 fusion.60
  347.6 3.9 fusion.64
  351.4 5.1 fusion.140
  358.5 3.6 collective-permute-start.7
  365.3 644.0 %reduce-scatter.2.cloned.1.call-done = f32[4,8,1024]{2,1,0:T(8,128)} async-done(((f32[4,1024,1024]{2,1,0:T(8,128)}), f32[4,8,1024]{2,1,0:T(8,128)}) %reduce-scatter.2.cloned.1.call-update) | async-done | bytes 131088 | tf_op jit(solution)/shard_map/reduce_scatter | solution.py:224
  (216 shorter events, 208.7 us)
Async XLA Ops:
  7.2 27.6 %copy-start.11 = (bf16[1,48,1024]{2,1,0:T(8,128)(2,1)S(1)}, bf16[1,48,1024]{2,1,0:T(8,128)(2,1)}, u32[]{:S(2)}) copy-start(bf16[1,48,1024]{2,1,0:T(8,128)(2,1)} %param.12) | copy-start | bytes 294916
  7.2 1002.2 %reduce-scatter.2.cloned.1.call-start = ((), (), s32[]{:S(2)}) async-start(), calls=%async_computation.1 | async-start | bytes 16908288 | tf_op jit(solution)/shard_map/reduce_scatter | solution.py:224
  7.2 27.6 %collective-permute-start.1 = (bf16[48,1024]{1,0:T(8,128)(2,1)}, bf16[48,1024]{1,0:T(8,128)(2,1)S(1)}, u32[]{:S(2)}, u32[]{:S(2)}) collective-permute-start(bf16[48,1024]{1,0:T(8,128)(2,1)} %bitcast.219), channel_id=1, source_target_pairs={{1,0},{2,1},{3,2},{4,3},{5,4},{6,5},{7,6},{8,7},{9,8},{10,9},{11,1... | collective-permute-start | bytes 294920 | tf_op jit(solution)/shard_map/ppermute | solution.py:22
  10.6 24.2 %collective-permute-start = (bf16[48,1024]{1,0:T(8,128)(2,1)}, bf16[48,1024]{1,0:T(8,128)(2,1)S(1)}, u32[]{:S(2)}, u32[]{:S(2)}) collective-permute-start(bf16[48,1024]{1,0:T(8,128)(2,1)} %bitcast.220), channel_id=1, source_target_pairs={{0,1},{1,2},{2,3},{3,4},{4,5},{5,6},{6,7},{7,8},{8,9},{9,10},{10,1... | collective-permute-start | bytes 294920 | tf_op jit(solution)/shard_map/ppermute | solution.py:20
  35.2 2.9 copy-start.6
  40.7 8.5 copy-start.2
  42.3 16.8 %collective-permute-start.2 = (bf16[256,2048]{1,0:T(8,128)(2,1)}, bf16[256,2048]{1,0:T(8,128)(2,1)S(1)}, u32[]{:S(2)}, u32[]{:S(2)}) collective-permute-start(bf16[256,2048]{1,0:T(8,128)(2,1)} %get-tuple-element.276), channel_id=1, source_target_pairs={{0,1},{1,2},{2,3},{3,4},{4,5},{5,6},{6,7},{7,8},{8,9},{9,10},{10,1... | collective-permute-start | bytes 3145736 | tf_op jit(solution)/shard_map/ppermute | solution.py:20
  47.0 16.4 %collective-permute-start.3 = (bf16[256,2048]{1,0:T(8,128)(2,1)}, bf16[256,2048]{1,0:T(8,128)(2,1)}, u32[]{:S(2)}, u32[]{:S(2)}) collective-permute-start(bf16[256,2048]{1,0:T(8,128)(2,1)} %get-tuple-element.277), channel_id=1, source_target_pairs={{1,0},{2,1},{3,2},{4,3},{5,4},{6,5},{7,6},{8,7},{9,8},{10,9},{11,1... | collective-permute-start | bytes 3145736 | tf_op jit(solution)/shard_map/ppermute | solution.py:22
  83.4 58.1 %copy-start.7 = (bf16[384,1024]{1,0:T(8,128)(2,1)S(1)}, bf16[384,1024]{1,0:T(8,128)(2,1)}, u32[]{:S(2)}) copy-start(bf16[384,1024]{1,0:T(8,128)(2,1)} %copy-done.6) | copy-start | bytes 2359300
  144.1 1.1 copy-start.3
  311.6 8.9 copy-start.1
  315.3 5.2 copy-start
  315.5 13.9 %collective-permute-start.4 = (bf16[256,2048]{0,1:T(8,128)(2,1)S(1)}, bf16[256,2048]{0,1:T(8,128)(2,1)S(1)}, u32[]{:S(2)}, u32[]{:S(2)}) collective-permute-start(bf16[256,2048]{0,1:T(8,128)(2,1)S(1)} %get-tuple-element.273), channel_id=1, source_target_pairs={{0,1},{1,2},{2,3},{3,4},{4,5},{5,6},{6,7},{7,8},{8,9},{9,10},{10,1... | collective-permute-start | bytes 3145736 | tf_op jit(solution)/shard_map/ppermute | solution.py:32
  317.7 3.1 copy-start.8
  317.7 3.1 copy-start.9
  317.7 16.2 %collective-permute-start.5 = (bf16[256,2048]{0,1:T(8,128)(2,1)S(1)}, bf16[256,2048]{0,1:T(8,128)(2,1)S(1)}, u32[]{:S(2)}, u32[]{:S(2)}) collective-permute-start(bf16[256,2048]{0,1:T(8,128)(2,1)S(1)} %get-tuple-element.272), channel_id=1, source_target_pairs={{1,0},{2,1},{3,2},{4,3},{5,4},{6,5},{7,6},{8,7},{9,8},{10,9},{11,1... | collective-permute-start | bytes 3145736 | tf_op jit(solution)/shard_map/ppermute | solution.py:32
  334.5 1.3 copy-start.4
  343.4 4.1 copy-start.5
  347.6 3.9 copy-start.10
  356.5 6.5 collective-permute-start.6
  358.5 5.3 collective-permute-start.7
Sparse Core Ops, SparseCore 0:
  343.5 665.7 reduce-scatter.1
where the time goes:
time: 1030 us; the launch traced here: 1020 us
  waiting for transfers between devices  663 us (64%)
  matrix products  231 us (22%)
  other arithmetic  40.9 us (4%)
  local copies, waits for them, and re-layouts  26.9 us (3%)
  starting transfers between devices  24.3 us (2%)
  between operations  15.1 us (1%)
  blocking collectives  14.4 us (1%)
    reduce_scatter x1, waiting for transfers between devices, on_device(): lax.psum_scatter(grad_terms, ('grp', 'seq'), scatter_dimension=1, tiled=T...  644 us
    dot_general x32, matrix products, probabilities(): jnp.dot(head_q, head_k.T, preferred_element_type=jnp.float32) * score_scale  54.1 us
    dot_general x16, matrix products, backward_one_head(): d_values = jnp.dot(probs_low.T, head_g, preferred_element_type=jnp.float32)  32 us
    dot_general x16, matrix products, backward_one_head(): d_query = jnp.dot(d_low, head_k, preferred_element_type=jnp.float32)  30.7 us
    dot_general x16, matrix products, backward_one_head(): d_keys = jnp.dot(d_low.T, head_q, preferred_element_type=jnp.float32)  29.8 us
    dot_general x16, matrix products, backward_one_head(): d_probs = jnp.dot(head_g, head_v.T, preferred_element_type=jnp.float32)  25.6 us
    dot_general x16, matrix products, forward_one_head(): return jnp.dot(attn_probs, head_v, preferred_element_type=jnp.float32)  24.3 us
  transfers between devices with their start and end apart: 9, of which 7 were waited for; matrix products, arithmetic and copies ran while one was open for 3% of the time, Pallas kernels for 0%

commit v1 on v0

v1 whole, which is shorter than its diff:
```python
import functools
import math

import jax
import jax.numpy as jnp
import numpy as np
from jax import lax
from jax.experimental import pallas as pl
from jax.experimental.pallas import tpu as pltpu
from jax.sharding import PartitionSpec as P

MESH = pl.DeviceIdType.MESH
BF16 = jnp.bfloat16
F32 = jnp.float32

D = 1024
HEADS = 16
WINDOW = 512
HALF = WINDOW // 2
F_DEV = 384
P_DEV = 48
SEQ = 32
GRP = 4
FRAMES = SEQ * F_DEV
EXT = F_DEV + WINDOW
TILE = 128
SPAN = TILE + WINDOW
TILES = F_DEV // TILE
PAIRS = HEADS // 2
NEAR = 5 * P_DEV
NEAR_PAD = 256
GROUPS = 4
COLS = D // GROUPS
GRAD_SCALE = 1.0 / math.sqrt(GRP * FRAMES)


def nn(a, b):
    return lax.dot_general(a, b, (((1,), (0,)), ((), ())), preferred_element_type=F32)


def nt(a, b):
    return lax.dot_general(a, b, (((1,), (1,)), ((), ())), preferred_element_type=F32)


def position_tables():
    half = D // 2
    rates = np.exp(np.arange(half) * (-math.log(10000.0) / half))
    tiles = SEQ * TILES + 2 * (HALF // TILE)
    coarse = (np.arange(tiles)[:, None] * TILE - HALF) * rates[None, :]
    fine = np.arange(TILE)[:, None] * rates[None, :]
    coarse = np.concatenate([np.sin(coarse), np.cos(coarse)], axis=1)
    fine = np.concatenate([np.sin(fine), np.cos(fine)], axis=1)
    pad = -coarse.shape[0] % 8
    coarse = np.pad(coarse, ((0, pad), (0, 0)))
    return coarse.astype(np.float32), fine.astype(np.float32)


def make_inputs(seq, near, bounds, coarse, fine, x, xt, oh, oht):
    half = D // 2
    begins = bounds[0:1, :]
    ends = bounds[1:2, :]

    @pl.loop(0, EXT // TILE)
    def _(i):
        rows = pl.ds(pl.multiple_of(i * TILE, TILE), TILE)
        frame = lax.broadcasted_iota(jnp.int32, (TILE, NEAR_PAD), 0) + (seq * F_DEV - HALF + i * TILE)
        onehot = jnp.where((frame >= begins) & (frame < ends), 1.0, 0.0)
        onehot_low = onehot.astype(BF16)
        oh[rows, :] = onehot_low
        expanded = nn(onehot_low, near[...])
        base = coarse[pl.ds(seq * TILES + i, 1), :]
        sin_a, cos_a = base[:, :half], base[:, half:]
        sin_b, cos_b = fine[:, :half], fine[:, half:]
        x[rows, :half] = (expanded[:, :half] + (sin_a * cos_b + cos_a * sin_b)).astype(BF16)
        x[rows, half:] = (expanded[:, half:] + (cos_a * cos_b - sin_a * sin_b)).astype(BF16)

    for i in range(EXT // TILE):
        rows = pl.ds(i * TILE, TILE)
        xt[:, rows] = x[rows, :].T
        oht[:, rows] = oh[rows, :].T


def make_projections(x, w, q, k, v, kt, vt):
    @pl.loop(0, D // 256)
    def _(n):
        cols = pl.ds(pl.multiple_of(n * 256, 256), 256)
        q[:, cols] = (nn(x[HALF : HALF + F_DEV, :], w[0, :, cols]).astype(BF16) * 0.125).astype(BF16)
        keys = nn(x[...], w[1, :, cols]).astype(BF16)
        k[:, cols] = keys
        kt[cols, :] = keys.T
        values = nn(x[...], w[2, :, cols]).astype(BF16)
        v[:, cols] = values
        vt[cols, :] = values.T


def make_bias(seq, bias):
    for i in range(TILES):
        key = lax.broadcasted_iota(jnp.int32, (SPAN, 2 * TILE), 0)
        query = lax.broadcasted_iota(jnp.int32, (SPAN, 2 * TILE), 1) % TILE
        frame = key + (seq * F_DEV - HALF + i * TILE)
        allowed = (key >= query) & (key < query + WINDOW) & (frame >= 0) & (frame < FRAMES)
        bias[i] = jnp.where(allowed, 0.0, -jnp.inf)


def two_heads(rows):
    lane = lax.broadcasted_iota(jnp.int32, rows.shape, 1)
    zero = jnp.zeros_like(rows)
    first = jnp.where(lane < 64, rows, zero)
    second = jnp.where(lane < 64, zero, rows)
    return jnp.concatenate([first, second], axis=0)


def own_halves(both):
    return jnp.concatenate([both[:64, :TILE], both[64:, TILE:]], axis=0)


def forward_attention(q, k, vt, bias, p, att_t):
    @pl.loop(0, PAIRS)
    def _(pair):
        cols = pl.ds(pl.multiple_of(pair * 128, 128), 128)
        for i in range(TILES):
            span = pl.ds(i * TILE, SPAN)
            rows = pl.ds(i * TILE, TILE)
            scores = nt(k[span, cols], two_heads(q[rows, cols])) + bias[i]
            peak = jnp.max(scores, axis=0, keepdims=True)
            raised = jnp.exp(scores - peak)
            total = jnp.sum(raised, axis=0, keepdims=True)
            probs = (raised * (1.0 / total)).astype(BF16)
            p[pair * TILES + i] = probs
            att_t[cols, rows] = own_halves(nn(vt[cols, span], probs)).astype(BF16)


def output_backward(x, att_t, d_out, w, d_proj, d_att):
    for i in range(TILES):
        rows = pl.ds(i * TILE, TILE)
        att = att_t[:, rows].T
        resid = x[HALF + i * TILE : HALF + (i + 1) * TILE, :].astype(F32) + nn(att, w[3])
        mean = jnp.mean(resid, axis=1, keepdims=True)
        centered = resid - mean
        inv_std = lax.rsqrt(jnp.mean(centered * centered, axis=1, keepdims=True) + 1e-5)
        normed = centered * inv_std
        cotan = d_out[rows, :].astype(F32)
        d_resid = inv_std * (
            cotan
            - jnp.mean(cotan, axis=1, keepdims=True)
            - normed * jnp.mean(cotan * normed, axis=1, keepdims=True)
        )
        d_proj[rows, :] = d_resid.astype(BF16)

    @pl.loop(0, D // 256)
    def _(n):
        cols = pl.ds(pl.multiple_of(n * 256, 256), 256)
        d_att[:, cols] = nt(d_proj[...], w[3, cols, :]).astype(BF16)


def backward_pair(pair, q, k, v, kt, d_att, p, dq_t, dk, dv, dk_sum, dv_sum):
    cols = pl.ds(pl.multiple_of(pair * 128, 128), 128)
    dk_sum[...] = jnp.zeros_like(dk_sum)
    dv_sum[...] = jnp.zeros_like(dv_sum)
    for i in range(TILES):
        span = pl.ds(i * TILE, SPAN)
        rows = pl.ds(i * TILE, TILE)
        both_q = two_heads(q[rows, cols])
        both_g = two_heads(d_att[rows, cols])
        probs_low = p[pair * TILES + i]
        d_probs = nt(v[span, cols], both_g)
        probs = probs_low.astype(F32)
        weighted = probs * d_probs
        delta = jnp.sum(weighted, axis=0, keepdims=True)
        d_low = (weighted - probs * delta).astype(BF16)
        dv_sum[span, :] += nn(probs_low, both_g)
        dk_sum[span, :] += nn(d_low, both_q)
        dq_t[cols, rows] = (own_halves(nn(kt[cols, span], d_low)) * 0.125).astype(BF16)
    dk[:, cols] = dk_sum[...].astype(BF16)
    dv[:, cols] = dv_sum[...].astype(BF16)


def blocks_of(product):
    count = product.shape[0] // 8
    cells = product.reshape(count, 8, COLS)
    return jnp.concatenate([cells[:, :, :128], cells[:, :, 128:]], axis=1).astype(BF16)


def split_cores(blocks):
    pairs = blocks.reshape(blocks.shape[0] // 2, 2, 16, 128)
    return pairs[:, 0], pairs[:, 1]


def weight_grad(product_of, store):
    for t in range(D // 256):
        first, second = split_cores(blocks_of(product_of(pl.ds(t * 256, 256))))
        store(0, t, first.reshape(4, 4, 16, 128))
        store(1, t, second.reshape(4, 4, 16, 128))


AXES = ("y", "x", "z")
ROTATIONS = (("z", "x", "y"), ("x", "y", "z"), ("y", "z", "x"))


def place():
    y = lax.axis_index("grp")
    seq = lax.axis_index("seq")
    return {"y": y, "x": seq // 8, "z": (seq // 2) % 4, "core": seq % 2, "seq": seq}


def device_of(at):
    return (at["y"], at["x"] * 8 + at["z"] * 2 + at["core"])


def along(at, axis, steps):
    moved = dict(at)
    moved[axis] = (at[axis] + steps) % 4
    return moved


def at_axis(ref, dims, axis, index):
    where = tuple(index if dim == axis else slice(None) for dim in dims)
    return ref.at[where]


class Reduction:
    def __init__(self, at, parts, from_core, sums, landed, core_sems, send_sems, recv_sems, turns):
        self.at, self.parts, self.from_core = at, parts, from_core
        self.sums, self.landed = (parts.at[at["core"]],) + sums, landed
        self.core_sems, self.send_sems, self.recv_sems = core_sems, send_sems, recv_sems
        self.turns = turns

    def core_copy(self):
        sibling = dict(self.at)
        sibling["core"] = 1 - self.at["core"]
        return pltpu.make_async_remote_copy(
            src_ref=self.parts.at[sibling["core"]],
            dst_ref=self.from_core,
            send_sem=self.core_sems.at[0],
            recv_sem=self.core_sems.at[1],
            device_id=device_of(sibling),
            device_id_type=MESH,
        )

    def axis_copy(self, stage, m, steps):
        order = ROTATIONS[self.turns[m]]
        axis = order[stage]
        dims = [dim for dim in AXES if dim not in order[:stage]]
        target = along(self.at, axis, steps)
        return pltpu.make_async_remote_copy(
            src_ref=at_axis(self.sums[stage].at[m], dims, axis, target[axis]),
            dst_ref=self.landed[stage].at[steps - 1, m],
            send_sem=self.send_sems.at[stage, m, steps - 1],
            recv_sem=self.recv_sems.at[stage, m, steps - 1],
            device_id=device_of(target),
            device_id_type=MESH,
        )

    def send_core(self):
        self.core_copy().start()

    def send_axis(self, stage):
        for m in range(len(self.turns)):
            for steps in (2, 1, 3):
                self.axis_copy(stage, m, steps).start()

    def first_sum(self):
        self.core_copy().wait_recv()
        for m in range(len(self.turns)):
            for y in range(4):
                total = self.sums[0][m, y].astype(F32) + self.from_core[m, y].astype(F32)
                self.sums[0][m, y] = total.astype(BF16)
        self.send_axis(0)

    def axis_total(self, stage, m):
        order = ROTATIONS[self.turns[m]]
        axis = order[stage]
        dims = [dim for dim in AXES if dim not in order[:stage]]
        for steps in (1, 3, 2):
            self.axis_copy(stage, m, steps).wait_recv()
        total = at_axis(self.sums[stage].at[m], dims, axis, self.at[axis])[...].astype(F32)
        for steps in (1, 2, 3):
            total = total + self.landed[stage][steps - 1, m].astype(F32)
        return total

    def next_sum(self, stage):
        for m in range(len(self.turns)):
            self.sums[stage][m] = self.axis_total(stage - 1, m).astype(BF16)
        self.send_axis(stage)

    def last_sum(self, put):
        for m in range(len(self.turns)):
            put(m, self.axis_total(2, m) * GRAD_SCALE)

    def drain(self):
        self.core_copy().wait_send()
        for stage in range(3):
            for m in range(len(self.turns)):
                for steps in (1, 2, 3):
                    self.axis_copy(stage, m, steps).wait_send()


def reduction_scratch(lead, n):
    return [
        pltpu.VMEM(lead + (2, n, 4, 4, 4, 16, 128), BF16),
        pltpu.VMEM(lead + (n, 4, 4, 4, 16, 128), BF16),
        pltpu.VMEM(lead + (n, 4, 4, 16, 128), BF16),
        pltpu.VMEM(lead + (n, 4, 16, 128), BF16),
        pltpu.VMEM(lead + (3, n, 4, 4, 16, 128), BF16),
        pltpu.VMEM(lead + (3, n, 4, 16, 128), BF16),
        pltpu.VMEM(lead + (3, n, 16, 128), BF16),
        pltpu.SemaphoreType.DMA(lead + (2,)),
        pltpu.SemaphoreType.DMA(lead + (3, n, 3)),
        pltpu.SemaphoreType.DMA(lead + (3, n, 3)),
    ]


def reduction_of(at, refs, turns):
    parts, from_core, s1, s2, l0, l1, l2, core_sems, send_sems, recv_sems = refs
    return Reduction(
        at, parts, from_core, (s1, s2), (l0, l1, l2), core_sems, send_sems, recv_sems, turns
    )


def greet(at):
    barrier = pltpu.get_barrier_semaphore()

    @pl.loop(1, SEQ)
    def _(steps):
        pl.semaphore_signal(
            barrier,
            inc=1,
            device_id=(at["y"], (at["seq"] + steps) % SEQ),
            device_id_type=MESH,
        )

    for steps in (1, 2, 3):
        pl.semaphore_signal(
            barrier, inc=1, device_id=device_of(along(at, "y", steps)), device_id_type=MESH
        )
    pl.semaphore_wait(barrier, SEQ - 1 + 3)


NEAR_STEPS = (1, -1, 2, -2)


def near_copy(at, phonemes, near, sems, i):
    steps = NEAR_STEPS[i]
    return pltpu.make_async_remote_copy(
        src_ref=phonemes.at[0],
        dst_ref=near.at[pl.ds((2 - steps) * P_DEV, P_DEV)],
        send_sem=sems.at[0, i],
        recv_sem=sems.at[1, i],
        device_id=(at["y"], (at["seq"] + steps + SEQ) % SEQ),
        device_id_type=MESH,
    )


def duration_copy(at, own, all_durations, sems, steps):
    return pltpu.make_async_remote_copy(
        src_ref=own,
        dst_ref=all_durations.at[at["seq"]],
        send_sem=sems.at[0],
        recv_sem=sems.at[1],
        device_id=(at["y"], (at["seq"] + steps) % SEQ),
        device_id_type=MESH,
    )


def make_bounds(seq, all_durations, rows, bounds):
    everyone = all_durations[:, 0, :]
    block_of = lax.broadcasted_iota(jnp.int32, (SEQ, 128), 0)
    rows[...] = jnp.zeros_like(rows)
    before = []
    for i in range(5):
        index = (seq + i - 2 + SEQ) % SEQ
        rows[i : i + 1, :] = all_durations[index][0:1, :]
        earlier = jnp.sum(jnp.where(block_of < index, everyone, 0), axis=0, keepdims=True)
        before.append(jnp.sum(earlier, axis=1, keepdims=True))
    lane = lax.broadcasted_iota(jnp.int32, (8, 128), 1)
    lengths = rows[...]
    running = lengths
    for shift in (1, 2, 4, 8, 16, 32):
        running = running + jnp.where(lane >= shift, pltpu.roll(running, shift, 1), 0)
    valid = lane < P_DEV
    ends = jnp.where(valid, running, 0)
    begins = jnp.where(valid, running - lengths, 0)
    empty = jnp.zeros((8, 128), jnp.int32)
    all_ends = jnp.zeros((1, 256), jnp.int32)
    all_begins = jnp.zeros((1, 256), jnp.int32)
    wide = lax.broadcasted_iota(jnp.int32, (1, 256), 1)
    for i in range(5):
        here = (wide >= i * P_DEV) & (wide < (i + 1) * P_DEV)
        end_row = jnp.concatenate([ends, empty], axis=1)
        begin_row = jnp.concatenate([begins, empty], axis=1)
        if i:
            end_row = pltpu.roll(end_row, i * P_DEV, 1)
            begin_row = pltpu.roll(begin_row, i * P_DEV, 1)
        all_ends = jnp.where(here, end_row[i : i + 1] + before[i], all_ends)
        all_begins = jnp.where(here, begin_row[i : i + 1] + before[i], all_begins)
    bounds[0:1, :] = all_begins
    bounds[1:2, :] = all_ends


def sum_copy(at, near_sums, landed, sems, i):
    steps = NEAR_STEPS[i]
    return pltpu.make_async_remote_copy(
        src_ref=near_sums.at[pl.ds((2 + steps) * P_DEV, P_DEV)],
        dst_ref=landed.at[i],
        send_sem=sems.at[0, i],
        recv_sem=sems.at[1, i],
        device_id=(at["y"], (at["seq"] + steps + SEQ) % SEQ),
        device_id_type=MESH,
    )


def phoneme_sums(oht, dq_t, dk, dv, d_proj, w, low_q, low_k, low_v, near_sums):
    own = pl.ds(HALF, F_DEV)

    @pl.loop(0, D // 256)
    def _(n):
        cols = pl.ds(pl.multiple_of(n * 256, 256), 256)
        low_q[:, cols] = nt(oht[:, own], dq_t[cols, :]).astype(BF16)
        low_k[:, cols] = nn(oht[...], dk[:, cols]).astype(BF16)
        low_v[:, cols] = nn(oht[...], dv[:, cols]).astype(BF16)

    @pl.loop(0, D // 256)
    def _(n):
        cols = pl.ds(pl.multiple_of(n * 256, 256), 256)
        total = nn(oht[:, own], d_proj[:, cols])
        total = total + nt(low_q[...], w[0, cols, :])
        total = total + nt(low_k[...], w[1, cols, :])
        total = total + nt(low_v[...], w[2, cols, :])
        near_sums[:, cols] = total.astype(BF16)


def kernel(
    phonemes, durations, weights, d_out, coarse, fine, d_phon, d_weights, *scratch
):
    (
        w, cotan, dur_own, dur_all, dur_rows, bounds, near, x, xt, oh, oht, q, k, v, kt, vt,
        bias, p, att_t, d_proj, d_att, dq_t, dk, dv, dk_sum, dv_sum, sums_landed, load_sems, dur_sems, near_sems, sum_sems, *rest
    ) = scratch
    out_refs, qkv_refs = rest[: len(rest) // 2], rest[len(rest) // 2 :]
    at = place()
    seq = at["seq"]

    loads = [pltpu.make_async_copy(weights.at[m], w.at[m], load_sems.at[m]) for m in range(4)]
    loads.append(pltpu.make_async_copy(d_out.at[0], cotan, load_sems.at[4]))
    for load in loads:
        load.start()

    dur_own[...] = jnp.zeros_like(dur_own)
    dur_own[0:1, 0:P_DEV] = durations[...]
    dur_all[seq] = dur_own[...]
    near[2 * P_DEV : 3 * P_DEV, :] = phonemes[0]
    near[NEAR:, :] = jnp.zeros((NEAR_PAD - NEAR, D), BF16)

    greet(at)

    @pl.loop(1, SEQ)
    def _(steps):
        duration_copy(at, dur_own, dur_all, dur_sems, steps).start()

    for i in range(4):
        near_copy(at, phonemes, near, near_sems, i).start()
    make_bias(seq, bias)

    others = dur_all.at[pl.ds(0, SEQ - 1)]
    pltpu.make_async_copy(others, others, dur_sems.at[1]).wait()
    make_bounds(seq, dur_all, dur_rows, bounds)
    for i in range(4):
        near_copy(at, phonemes, near, near_sems, i).wait_recv()

    make_inputs(seq, near, bounds, coarse, fine, x, xt, oh, oht)
    for m in range(3):
        loads[m].wait()
    make_projections(x, w, q, k, v, kt, vt)
    forward_attention(q, k, vt, bias, p, att_t)
    loads[3].wait()
    loads[4].wait()
    output_backward(x, att_t, cotan, w, d_proj, d_att)

    out_turn = reduction_of(at, out_refs, (0, 1, 2, 0))
    for j in range(GROUPS):
        cols = pl.ds(j * COLS, COLS)

        def store(core, block, value):
            out_refs[0][core, j, block] = value

        weight_grad(lambda rows: nn(att_t[rows, :], d_proj[:, cols]), store)
    out_turn.send_core()

    turns = [
        reduction_of(at, [ref.at[g] for ref in qkv_refs], (0, 1, 2)) for g in range(GROUPS)
    ]

    def put_out(m, total):
        cols = m * COLS
        d_weights[3, :, cols : cols + 128] = total[:8]
        d_weights[3, :, cols + 128 : cols + COLS] = total[8:]

    def steps_of(turn, put):
        return [
            turn.first_sum,
            lambda: turn.next_sum(1),
            lambda: turn.next_sum(2),
            lambda: turn.last_sum(put),
        ]

    def put_of(g):
        def put(m, total):
            cols = g * COLS
            d_weights[m, :, cols : cols + 128] = total[:8]
            d_weights[m, :, cols + 128 : cols + COLS] = total[8:]

        return put

    pending = steps_of(out_turn, put_out)
    for g in range(GROUPS):
        for half in range(2):
            backward_pair(
                g * 2 + half, q, k, v, kt, d_att, p, dq_t, dk, dv, dk_sum, dv_sum
            )
            for _ in range(2):
                if pending:
                    pending.pop(0)()
        cols = pl.ds(g * COLS, COLS)
        own = pl.ds(HALF, F_DEV)
        products = [
            lambda rows: nt(xt[rows, own], dq_t[cols, :]),
            lambda rows: nn(xt[rows, :], dk[:, cols]),
            lambda rows: nn(xt[rows, :], dv[:, cols]),
        ]
        for m in range(3):

            def store(core, block, value):
                qkv_refs[0][g, core, m, block] = value

            weight_grad(products[m], store)
        turns[g].send_core()
        pending = steps_of(turns[g], put_of(g))

    pending.pop(0)()
    near_sums = near
    low_q, low_k, low_v = [x.at[pl.ds(m * NEAR_PAD, NEAR_PAD)] for m in range(3)]
    phoneme_sums(oht, dq_t, dk, dv, d_proj, w, low_q, low_k, low_v, near_sums)
    for i in range(4):
        sum_copy(at, near_sums, sums_landed, sum_sems, i).start()
    for step in pending:
        step()
    total = near_sums[2 * P_DEV : 3 * P_DEV, :].astype(F32)
    for i in range(4):
        sum_copy(at, near_sums, sums_landed, sum_sems, i).wait_recv()
        total = total + sums_landed[i].astype(F32)
    d_phon[0] = total.astype(BF16)

    pltpu.make_async_copy(others, others, dur_sems.at[0]).wait()
    for i in range(4):
        near_copy(at, phonemes, near, near_sems, i).wait_send()
        sum_copy(at, near_sums, sums_landed, sum_sems, i).wait_send()
    out_turn.drain()
    for turn in turns:
        turn.drain()


def on_device(phonemes, durations, weights, d_out):
    coarse, fine = position_tables()
    vmem = pl.BlockSpec(memory_space=pltpu.VMEM)
    hbm = pl.BlockSpec(memory_space=pl.ANY)
    scratch = [
        pltpu.VMEM((4, D, D), BF16),
        pltpu.VMEM((F_DEV, D), BF16),
        pltpu.VMEM((8, 128), jnp.int32),
        pltpu.VMEM((SEQ, 8, 128), jnp.int32),
        pltpu.VMEM((8, 128), jnp.int32),
        pltpu.VMEM((8, NEAR_PAD), jnp.int32),
        pltpu.VMEM((NEAR_PAD, D), BF16),
        pltpu.VMEM((EXT, D), BF16),
        pltpu.VMEM((D, EXT), BF16),
        pltpu.VMEM((EXT, NEAR_PAD), BF16),
        pltpu.VMEM((NEAR_PAD, EXT), BF16),
        pltpu.VMEM((F_DEV, D), BF16),
        pltpu.VMEM((EXT, D), BF16),
        pltpu.VMEM((EXT, D), BF16),
        pltpu.VMEM((D, EXT), BF16),
        pltpu.VMEM((D, EXT), BF16),
        pltpu.VMEM((TILES, SPAN, 2 * TILE), F32),
        pltpu.VMEM((PAIRS * TILES, SPAN, 2 * TILE), BF16),
        pltpu.VMEM((D, F_DEV), BF16),
        pltpu.VMEM((F_DEV, D), BF16),
        pltpu.VMEM((F_DEV, D), BF16),
        pltpu.VMEM((D, F_DEV), BF16),
        pltpu.VMEM((EXT, D), BF16),
        pltpu.VMEM((EXT, D), BF16),
        pltpu.VMEM((EXT, 128), F32),
        pltpu.VMEM((EXT, 128), F32),
        pltpu.VMEM((4, P_DEV, D), BF16),
        pltpu.SemaphoreType.DMA((5,)),
        pltpu.SemaphoreType.DMA((2,)),
        pltpu.SemaphoreType.DMA((2, 4)),
        pltpu.SemaphoreType.DMA((2, 4)),
    ]
    scratch += reduction_scratch((), 4)
    scratch += reduction_scratch((GROUPS,), 3)
    return pl.pallas_call(
        kernel,
        out_shape=(
            jax.ShapeDtypeStruct((1, P_DEV, D), BF16),
            jax.ShapeDtypeStruct((4, 8, D), F32),
        ),
        in_specs=[vmem, vmem, hbm, hbm, vmem, vmem],
        out_specs=(vmem, vmem),
        scratch_shapes=scratch,
        compiler_params=pltpu.CompilerParams(
            collective_id=0, has_side_effects=True, vmem_limit_bytes=62 * 1024 * 1024
        ),
    )(phonemes, durations, weights, d_out, coarse, fine)


def solution(mesh):
    return jax.shard_map(
        on_device,
        mesh=mesh,
        in_specs=(P("grp", "seq", None), P("grp", "seq"), P(), P("grp", "seq", None)),
        out_specs=(P("grp", "seq", None), P(None, ("grp", "seq"), None)),
        check_vma=False,
    )
```

time: 1030 us -> 138 us (0.13); the launches traced: 1020 us -> 137 us
  waiting for transfers between devices: 663 us -> 0 us
  matrix products: 231 us -> 0 us
  Pallas kernels: 0 us -> 134 us
  other arithmetic: 40.9 us -> 0 us
  starting transfers between devices: 24.3 us -> 0 us
  local copies, waits for them, and re-layouts: 26.9 us -> 3.11 us
  between operations: 15.1 us -> 0.64 us
  blocking collectives: 14.4 us -> 0 us
    reduce_scatter x1 -> x0, waiting for transfers between devices: 644 us -> none  [on_device(): lax.psum_scatter(grad_terms, ('grp', 'seq'), scatter_dimension=1, tiled=T...]
    dot_general x125 -> x0, matrix products: 231 us -> none  [the longest x32 54.1 us: probabilities(): jnp.dot(head_q, head_k.T, preferred_element_type=jnp.float32) * score_scale]
    pallas_call x0 -> x1, Pallas kernels: none -> 134 us  [on_device(): pl.pallas_call(kernel, out_shape=(jax.ShapeDtypeStruct((1, P_DEV, D), BF1...]
    ppermute x8 -> x0, starting transfers between devices: 24.3 us -> none  [the longest x4 10.6 us: shifted(): lax.ppermute(value, axis, [(source, source + steps) for source in range(l...]
    ppermute x8 -> x0, waiting for transfers between devices: 19.1 us -> none  [the longest x4 11.8 us: shifted(): lax.ppermute(value, axis, [(source, source + steps) for source in range(l...]
    all_gather x1 -> x0, blocking collectives: 14.4 us -> none  [on_device(): all_lengths = lax.all_gather(lengths, 'seq', axis=0, tiled=True)]
    reduce_sum x35 -> x0, other arithmetic: 13.7 us -> none  [the longest x32 12.8 us: probabilities(): return exp_scores / jnp.sum(exp_scores, axis=1, keepdims=True)]
    unnamed x30 -> x2, local copies, waits for them, and re-layouts: 13.6 us -> 3.11 us
  transfers between devices with their start and end apart: 9 -> 0, of which waited for: 7 -> 0; matrix products, arithmetic and copies ran while one was open for 3% -> 0% of each run, Pallas kernels for 0% -> 0%
where the time goes in v1:
time: 138 us; the launch traced here: 137 us
  Pallas kernels  134 us (97%)
  local copies, waits for them, and re-layouts  3.11 us (2%)
    pallas_call x1, Pallas kernels, on_device(): pl.pallas_call(kernel, out_shape=(jax.ShapeDtypeStruct((1, P_DEV, D), BF1...  134 us
    unnamed x2, local copies, waits for them, and re-layouts  3.11 us

profile of v1, /device:TPU:1, one launch (start us, length us, event | category | flops | bytes accessed | tf_op | source)
XLA Modules:
  0.0 137.5 jit_solution(15557084550009726893)
XLA Ops:
  0.6 133.7 %shard_map.77 = (bf16[1,48,1024]{2,1,0:T(8,128)(2,1)}, f32[4,8,1024]{2,1,0:T(8,128)}) custom-call(bf16[1,48,1024]{2,1,0:T(8,128)(2,1)} %phonemes.1, s32[1,48]{1,0:T(1,128)} %durations.1, bf16[4,1024,1024]{2,1,0:T(8,128)(2,1)} %weights.1, bf16[1,384,1024]{2,1,0:T(8,128)(2,1)} %d_out.1, f32[104,1024]{1,0:T(8,128)} %constant.4.clone.coarse, ...), custom_call_target="tpu_custom_call" | custom-call | tf_op jit(solution)/shard_map/pallas_call | solution.py:601
  134.4 1.5 %copy.10 = bf16[1,48,1024]{2,1,0:T(8,128)(2,1)} copy(bf16[1,48,1024]{2,1,0:T(8,128)(2,1)} %get-tuple-element.4) | data formatting | bytes 196608
  135.9 1.6 %copy.11 = f32[4,8,1024]{2,1,0:T(8,128)} copy(f32[4,8,1024]{2,1,0:T(8,128)} %get-tuple-element.5) | data formatting | bytes 262144

commit v2 on v1

--- a/solution.py
+++ b/solution.py
@@ -55,7 +55,7 @@
     return coarse.astype(np.float32), fine.astype(np.float32)
 
 
-def make_inputs(seq, near, bounds, coarse, fine, x, xt, oh, oht):
+def make_inputs(seq, near, bounds, coarse, fine, x, xt, oht):
     half = D // 2
     begins = bounds[0:1, :]
     ends = bounds[1:2, :]
@@ -66,7 +66,7 @@
         frame = lax.broadcasted_iota(jnp.int32, (TILE, NEAR_PAD), 0) + (seq * F_DEV - HALF + i * TILE)
         onehot = jnp.where((frame >= begins) & (frame < ends), 1.0, 0.0)
         onehot_low = onehot.astype(BF16)
-        oh[rows, :] = onehot_low
+        oht[:, rows] = onehot_low.T
         expanded = nn(onehot_low, near[...])
         base = coarse[pl.ds(seq * TILES + i, 1), :]
         sin_a, cos_a = base[:, :half], base[:, half:]
@@ -77,7 +77,6 @@
     for i in range(EXT // TILE):
         rows = pl.ds(i * TILE, TILE)
         xt[:, rows] = x[rows, :].T
-        oht[:, rows] = oh[rows, :].T
 
 
 def make_projections(x, w, q, k, v, kt, vt):
@@ -115,8 +114,7 @@
 
 
 def forward_attention(q, k, vt, bias, p, att_t):
-    @pl.loop(0, PAIRS)
-    def _(pair):
+    def make_probs(pair):
         cols = pl.ds(pl.multiple_of(pair * 128, 128), 128)
         for i in range(TILES):
             span = pl.ds(i * TILE, SPAN)
@@ -125,12 +123,26 @@
             peak = jnp.max(scores, axis=0, keepdims=True)
             raised = jnp.exp(scores - peak)
             total = jnp.sum(raised, axis=0, keepdims=True)
-            probs = (raised * (1.0 / total)).astype(BF16)
-            p[pair * TILES + i] = probs
-            att_t[cols, rows] = own_halves(nn(vt[cols, span], probs)).astype(BF16)
-
-
-def output_backward(x, att_t, d_out, w, d_proj, d_att):
+            p[pair * TILES + i] = (raised * (1.0 / total)).astype(BF16)
+
+    def attend(pair):
+        cols = pl.ds(pl.multiple_of(pair * 128, 128), 128)
+        for i in range(TILES):
+            span = pl.ds(i * TILE, SPAN)
+            rows = pl.ds(i * TILE, TILE)
+            att_t[cols, rows] = own_halves(nn(vt[cols, span], p[pair * TILES + i])).astype(BF16)
+
+    make_probs(0)
+
+    @pl.loop(1, PAIRS)
+    def _(pair):
+        attend(pair - 1)
+        make_probs(pair)
+
+    attend(PAIRS - 1)
+
+
+def output_backward(x, att_t, d_out, w, d_proj):
     for i in range(TILES):
         rows = pl.ds(i * TILE, TILE)
         att = att_t[:, rows].T
@@ -147,32 +159,60 @@
         )
         d_proj[rows, :] = d_resid.astype(BF16)
 
+
+def attended_grads(w, d_proj, d_att):
     @pl.loop(0, D // 256)
     def _(n):
         cols = pl.ds(pl.multiple_of(n * 256, 256), 256)
         d_att[:, cols] = nt(d_proj[...], w[3, cols, :]).astype(BF16)
 
 
-def backward_pair(pair, q, k, v, kt, d_att, p, dq_t, dk, dv, dk_sum, dv_sum):
-    cols = pl.ds(pl.multiple_of(pair * 128, 128), 128)
-    dk_sum[...] = jnp.zeros_like(dk_sum)
-    dv_sum[...] = jnp.zeros_like(dv_sum)
+def score_grads(pair, v, d_att, p, ds):
+    cols = pl.ds(pair * 128, 128)
     for i in range(TILES):
-        span = pl.ds(i * TILE, SPAN)
-        rows = pl.ds(i * TILE, TILE)
-        both_q = two_heads(q[rows, cols])
-        both_g = two_heads(d_att[rows, cols])
-        probs_low = p[pair * TILES + i]
-        d_probs = nt(v[span, cols], both_g)
-        probs = probs_low.astype(F32)
+        both_g = two_heads(d_att[i * TILE : (i + 1) * TILE, cols])
+        d_probs = nt(v[pl.ds(i * TILE, SPAN), cols], both_g)
+        probs = p[pair * TILES + i].astype(F32)
         weighted = probs * d_probs
         delta = jnp.sum(weighted, axis=0, keepdims=True)
-        d_low = (weighted - probs * delta).astype(BF16)
-        dv_sum[span, :] += nn(probs_low, both_g)
-        dk_sum[span, :] += nn(d_low, both_q)
-        dq_t[cols, rows] = (own_halves(nn(kt[cols, span], d_low)) * 0.125).astype(BF16)
-    dk[:, cols] = dk_sum[...].astype(BF16)
-    dv[:, cols] = dv_sum[...].astype(BF16)
+        ds[pair % 2, i] = (weighted - probs * delta).astype(BF16)
+
+
+def key_sums(cells, rights, put):
+    first, second, third = rights
+    middle = jnp.concatenate([cells(0, 256, 640), cells(1, 128, 512), cells(2, 0, 384)], axis=1)
+    put(256, nn(middle, jnp.concatenate([first, second, third], axis=0)))
+    put(0, nn(cells(0, 0, 128), first))
+    near = jnp.concatenate([cells(0, 128, 256), cells(1, 0, 128)], axis=1)
+    put(128, nn(near, jnp.concatenate([first, second], axis=0)))
+    far = jnp.concatenate([cells(1, 512, 640), cells(2, 384, 512)], axis=1)
+    put(640, nn(far, jnp.concatenate([second, third], axis=0)))
+    put(768, nn(cells(2, 512, 640), third))
+
+
+def pair_grads(pair, q, kt, d_att, p, ds, dq_t, dk, dv):
+    cols = pl.ds(pair * 128, 128)
+    tiles = [pl.ds(i * TILE, TILE) for i in range(TILES)]
+
+    def put_keys(row, value):
+        dk[pl.ds(row, value.shape[0]), cols] = value.astype(BF16)
+
+    def put_values(row, value):
+        dv[pl.ds(row, value.shape[0]), cols] = value.astype(BF16)
+
+    for i in range(TILES):
+        both = nn(kt[cols, pl.ds(i * TILE, SPAN)], ds[pair % 2, i])
+        dq_t[cols, tiles[i]] = (own_halves(both) * 0.125).astype(BF16)
+    key_sums(
+        lambda i, begin, end: ds[pair % 2, i, begin:end, :],
+        [two_heads(q[rows, cols]) for rows in tiles],
+        put_keys,
+    )
+    key_sums(
+        lambda i, begin, end: p[pair * TILES + i, begin:end, :],
+        [two_heads(d_att[rows, cols]) for rows in tiles],
+        put_values,
+    )
 
 
 def blocks_of(product):
@@ -333,7 +373,10 @@
         pl.semaphore_signal(
             barrier, inc=1, device_id=device_of(along(at, "y", steps)), device_id_type=MESH
         )
-    pl.semaphore_wait(barrier, SEQ - 1 + 3)
+
+
+def await_greetings():
+    pl.semaphore_wait(pltpu.get_barrier_semaphore(), SEQ - 1 + 3)
 
 
 NEAR_STEPS = (1, -1, 2, -2)
@@ -409,7 +452,7 @@
     )
 
 
-def phoneme_sums(oht, dq_t, dk, dv, d_proj, w, low_q, low_k, low_v, near_sums):
+def phoneme_low(oht, dq_t, dk, dv, low_q, low_k, low_v):
     own = pl.ds(HALF, F_DEV)
 
     @pl.loop(0, D // 256)
@@ -418,6 +461,10 @@
         low_q[:, cols] = nt(oht[:, own], dq_t[cols, :]).astype(BF16)
         low_k[:, cols] = nn(oht[...], dk[:, cols]).astype(BF16)
         low_v[:, cols] = nn(oht[...], dv[:, cols]).astype(BF16)
+
+
+def phoneme_sums(oht, d_proj, w, low_q, low_k, low_v, near_sums):
+    own = pl.ds(HALF, F_DEV)
 
     @pl.loop(0, D // 256)
     def _(n):
@@ -430,28 +477,35 @@
 
 
 def kernel(
-    phonemes, durations, weights, d_out, coarse, fine, d_phon, d_weights, *scratch
+    phonemes, durations, weights, d_out, coarse_in, fine_in, d_phon, d_weights, *scratch
 ):
     (
-        w, cotan, dur_own, dur_all, dur_rows, bounds, near, x, xt, oh, oht, q, k, v, kt, vt,
-        bias, p, att_t, d_proj, d_att, dq_t, dk, dv, dk_sum, dv_sum, sums_landed, load_sems, dur_sems, near_sems, sum_sems, *rest
+        w, cotan, coarse, fine, dur_own, dur_all, dur_rows, bounds, near, x, xt, oht, q, k, v, kt, vt,
+        bias, p, att_t, d_proj, dq_t, dk, dv, ds, sums_landed, load_sems, dur_sems, near_sems, sum_sems, *rest
     ) = scratch
     out_refs, qkv_refs = rest[: len(rest) // 2], rest[len(rest) // 2 :]
+    d_att = cotan
     at = place()
     seq = at["seq"]
 
+    greet(at)
+    tables = [
+        pltpu.make_async_copy(coarse_in, coarse, load_sems.at[5]),
+        pltpu.make_async_copy(fine_in, fine, load_sems.at[6]),
+        pltpu.make_async_copy(
+            phonemes.at[0], near.at[pl.ds(2 * P_DEV, P_DEV)], load_sems.at[7]
+        ),
+    ]
     loads = [pltpu.make_async_copy(weights.at[m], w.at[m], load_sems.at[m]) for m in range(4)]
     loads.append(pltpu.make_async_copy(d_out.at[0], cotan, load_sems.at[4]))
-    for load in loads:
+    for load in tables + loads[:3]:
         load.start()
 
     dur_own[...] = jnp.zeros_like(dur_own)
     dur_own[0:1, 0:P_DEV] = durations[...]
     dur_all[seq] = dur_own[...]
-    near[2 * P_DEV : 3 * P_DEV, :] = phonemes[0]
     near[NEAR:, :] = jnp.zeros((NEAR_PAD - NEAR, D), BF16)
-
-    greet(at)
+    await_greetings()
 
     @pl.loop(1, SEQ)
     def _(steps):
@@ -459,6 +513,8 @@
 
     for i in range(4):
         near_copy(at, phonemes, near, near_sems, i).start()
+    for load in loads[3:]:
+        load.start()
     make_bias(seq, bias)
 
     others = dur_all.at[pl.ds(0, SEQ - 1)]
@@ -466,26 +522,19 @@
     make_bounds(seq, dur_all, dur_rows, bounds)
     for i in range(4):
         near_copy(at, phonemes, near, near_sems, i).wait_recv()
-
-    make_inputs(seq, near, bounds, coarse, fine, x, xt, oh, oht)
+    for load in tables:
+        load.wait()
+
+    make_inputs(seq, near, bounds, coarse, fine, x, xt, oht)
     for m in range(3):
         loads[m].wait()
     make_projections(x, w, q, k, v, kt, vt)
     forward_attention(q, k, vt, bias, p, att_t)
     loads[3].wait()
     loads[4].wait()
-    output_backward(x, att_t, cotan, w, d_proj, d_att)
+    output_backward(x, att_t, cotan, w, d_proj)
 
     out_turn = reduction_of(at, out_refs, (0, 1, 2, 0))
-    for j in range(GROUPS):
-        cols = pl.ds(j * COLS, COLS)
-
-        def store(core, block, value):
-            out_refs[0][core, j, block] = value
-
-        weight_grad(lambda rows: nn(att_t[rows, :], d_proj[:, cols]), store)
-    out_turn.send_core()
-
     turns = [
         reduction_of(at, [ref.at[g] for ref in qkv_refs], (0, 1, 2)) for g in range(GROUPS)
     ]
@@ -494,14 +543,6 @@
         cols = m * COLS
         d_weights[3, :, cols : cols + 128] = total[:8]
         d_weights[3, :, cols + 128 : cols + COLS] = total[8:]
-
-    def steps_of(turn, put):
-        return [
-            turn.first_sum,
-            lambda: turn.next_sum(1),
-            lambda: turn.next_sum(2),
-            lambda: turn.last_sum(put),
-        ]
 
     def put_of(g):
         def put(m, total):
@@ -511,15 +552,16 @@
 
         return put
 
-    pending = steps_of(out_turn, put_out)
-    for g in range(GROUPS):
-        for half in range(2):
-            backward_pair(
-                g * 2 + half, q, k, v, kt, d_att, p, dq_t, dk, dv, dk_sum, dv_sum
-            )
-            for _ in range(2):
-                if pending:
-                    pending.pop(0)()
+    def out_grads():
+        for j in range(GROUPS):
+            cols = pl.ds(j * COLS, COLS)
+
+            def store(core, y, value):
+                out_refs[0][core, j, y] = value
+
+            weight_grad(lambda rows: nn(att_t[rows, :], d_proj[:, cols]), store)
+
+    def group_grads(g):
         cols = pl.ds(g * COLS, COLS)
         own = pl.ds(HALF, F_DEV)
         products = [
@@ -529,26 +571,72 @@
         ]
         for m in range(3):
 
-            def store(core, block, value):
-                qkv_refs[0][g, core, m, block] = value
+            def store(core, y, value):
+                qkv_refs[0][g, core, m, y] = value
 
             weight_grad(products[m], store)
-        turns[g].send_core()
-        pending = steps_of(turns[g], put_of(g))
-
-    pending.pop(0)()
+
+    def both_phases(pair):
+        if pair + 1 < PAIRS:
+            score_grads(pair + 1, v, d_att, p, ds)
+        pair_grads(pair, q, kt, d_att, p, ds, dq_t, dk, dv)
+
+    out_grads()
+    out_turn.send_core()
+    attended_grads(w, d_proj, d_att)
+
+    score_grads(0, v, d_att, p, ds)
+    both_phases(0)
+    both_phases(1)
+    group_grads(0)
+    turns[0].send_core()
+    out_turn.first_sum()
+
+    both_phases(2)
+    both_phases(3)
+    group_grads(1)
+    turns[1].send_core()
+    turns[0].first_sum()
+
+    both_phases(4)
+    both_phases(5)
+    group_grads(2)
+    turns[2].send_core()
+    turns[1].first_sum()
+    out_turn.next_sum(1)
+
+    both_phases(6)
+    both_phases(7)
+    group_grads(3)
+    turns[3].send_core()
+    turns[2].first_sum()
+    turns[0].next_sum(1)
+
     near_sums = near
     low_q, low_k, low_v = [x.at[pl.ds(m * NEAR_PAD, NEAR_PAD)] for m in range(3)]
-    phoneme_sums(oht, dq_t, dk, dv, d_proj, w, low_q, low_k, low_v, near_sums)
+    phoneme_low(oht, dq_t, dk, dv, low_q, low_k, low_v)
+    turns[3].first_sum()
+    turns[1].next_sum(1)
+    out_turn.next_sum(2)
+    phoneme_sums(oht, d_proj, w, low_q, low_k, low_v, near_sums)
     for i in range(4):
         sum_copy(at, near_sums, sums_landed, sum_sems, i).start()
-    for step in pending:
-        step()
+    turns[2].next_sum(1)
+    turns[0].next_sum(2)
+    turns[3].next_sum(1)
+    turns[1].next_sum(2)
+    out_turn.last_sum(put_out)
+    turns[2].next_sum(2)
+    turns[0].last_sum(put_of(0))
+    turns[3].next_sum(2)
+    turns[1].last_sum(put_of(1))
+    turns[2].last_sum(put_of(2))
     total = near_sums[2 * P_DEV : 3 * P_DEV, :].astype(F32)
     for i in range(4):
         sum_copy(at, near_sums, sums_landed, sum_sems, i).wait_recv()
         total = total + sums_landed[i].astype(F32)
     d_phon[0] = total.astype(BF16)
+    turns[3].last_sum(put_of(3))
 
     pltpu.make_async_copy(others, others, dur_sems.at[0]).wait()
     for i in range(4):
@@ -566,6 +654,8 @@
     scratch = [
         pltpu.VMEM((4, D, D), BF16),
         pltpu.VMEM((F_DEV, D), BF16),
+        pltpu.VMEM(coarse.shape, F32),
+        pltpu.VMEM(fine.shape, F32),
         pltpu.VMEM((8, 128), jnp.int32),
         pltpu.VMEM((SEQ, 8, 128), jnp.int32),
         pltpu.VMEM((8, 128), jnp.int32),
@@ -573,7 +663,6 @@
         pltpu.VMEM((NEAR_PAD, D), BF16),
         pltpu.VMEM((EXT, D), BF16),
         pltpu.VMEM((D, EXT), BF16),
-        pltpu.VMEM((EXT, NEAR_PAD), BF16),
         pltpu.VMEM((NEAR_PAD, EXT), BF16),
         pltpu.VMEM((F_DEV, D), BF16),
         pltpu.VMEM((EXT, D), BF16),
@@ -584,14 +673,12 @@
         pltpu.VMEM((PAIRS * TILES, SPAN, 2 * TILE), BF16),
         pltpu.VMEM((D, F_DEV), BF16),
         pltpu.VMEM((F_DEV, D), BF16),
-        pltpu.VMEM((F_DEV, D), BF16),
         pltpu.VMEM((D, F_DEV), BF16),
         pltpu.VMEM((EXT, D), BF16),
         pltpu.VMEM((EXT, D), BF16),
-        pltpu.VMEM((EXT, 128), F32),
-        pltpu.VMEM((EXT, 128), F32),
+        pltpu.VMEM((2, TILES, SPAN, 2 * TILE), BF16),
         pltpu.VMEM((4, P_DEV, D), BF16),
-        pltpu.SemaphoreType.DMA((5,)),
+        pltpu.SemaphoreType.DMA((8,)),
         pltpu.SemaphoreType.DMA((2,)),
         pltpu.SemaphoreType.DMA((2, 4)),
         pltpu.SemaphoreType.DMA((2, 4)),
@@ -604,7 +691,7 @@
             jax.ShapeDtypeStruct((1, P_DEV, D), BF16),
             jax.ShapeDtypeStruct((4, 8, D), F32),
         ),
-        in_specs=[vmem, vmem, hbm, hbm, vmem, vmem],
+        in_specs=[hbm, vmem, hbm, hbm, hbm, hbm],
         out_specs=(vmem, vmem),
         scratch_shapes=scratch,
         compiler_params=pltpu.CompilerParams(

time: 138 us -> 80.1 us (0.58)
  Pallas kernels: 134 us -> 76.2 us
    pallas_call x1, Pallas kernels: 134 us -> 76.2 us  [on_device(): pl.pallas_call(kernel, out_shape=(jax.ShapeDtypeStruct((1, P_DEV, D), BF1...]
where the time goes in v2:
time: 80.1 us; the launch traced here: 80 us
  Pallas kernels  76.2 us (95%)
  local copies, waits for them, and re-layouts  3.11 us (4%)
    pallas_call x1, Pallas kernels, on_device(): pl.pallas_call(kernel, out_shape=(jax.ShapeDtypeStruct((1, P_DEV, D), BF1...  76.2 us
    unnamed x2, local copies, waits for them, and re-layouts  3.11 us

profile of v2, /device:TPU:1, one launch (start us, length us, event | category | flops | bytes accessed | tf_op | source)
XLA Modules:
  0.0 80.0 jit_solution(10417299190613918883)
XLA Ops:
  0.6 76.2 %shard_map.77 = (bf16[1,48,1024]{2,1,0:T(8,128)(2,1)}, f32[4,8,1024]{2,1,0:T(8,128)}) custom-call(bf16[1,48,1024]{2,1,0:T(8,128)(2,1)} %phonemes.1, s32[1,48]{1,0:T(1,128)} %durations.1, bf16[4,1024,1024]{2,1,0:T(8,128)(2,1)} %weights.1, bf16[1,384,1024]{2,1,0:T(8,128)(2,1)} %d_out.1, f32[104,1024]{1,0:T(8,128)} %constant.4.clone.coarse_in, ...), custom_call_target="tpu_custom_call" | custom-call | tf_op jit(solution)/shard_map/pallas_call | solution.py:688
  76.9 1.5 %copy.10 = bf16[1,48,1024]{2,1,0:T(8,128)(2,1)} copy(bf16[1,48,1024]{2,1,0:T(8,128)(2,1)} %get-tuple-element.4) | data formatting | bytes 196608
  78.4 1.6 %copy.11 = f32[4,8,1024]{2,1,0:T(8,128)} copy(f32[4,8,1024]{2,1,0:T(8,128)} %get-tuple-element.5) | data formatting | bytes 262144

commit v3 on v2

--- a/solution.py
+++ b/solution.py
@@ -79,17 +79,16 @@
         xt[:, rows] = x[rows, :].T
 
 
-def make_projections(x, w, q, k, v, kt, vt):
-    @pl.loop(0, D // 256)
-    def _(n):
-        cols = pl.ds(pl.multiple_of(n * 256, 256), 256)
-        q[:, cols] = (nn(x[HALF : HALF + F_DEV, :], w[0, :, cols]).astype(BF16) * 0.125).astype(BF16)
-        keys = nn(x[...], w[1, :, cols]).astype(BF16)
-        k[:, cols] = keys
-        kt[cols, :] = keys.T
-        values = nn(x[...], w[2, :, cols]).astype(BF16)
-        v[:, cols] = values
-        vt[cols, :] = values.T
+def project_queries(n, x, w, q):
+    cols = pl.ds(pl.multiple_of(n * 256, 256), 256)
+    q[:, cols] = (nn(x[HALF : HALF + F_DEV, :], w[0, :, cols]).astype(BF16) * 0.125).astype(BF16)
+
+
+def project_extended(n, x, weight, out, out_t):
+    cols = pl.ds(pl.multiple_of(n * 256, 256), 256)
+    rows = nn(x[...], weight[:, cols]).astype(BF16)
+    out[:, cols] = rows
+    out_t[cols, :] = rows.T
 
 
 def make_bias(seq, bias):
@@ -113,33 +112,61 @@
     return jnp.concatenate([both[:64, :TILE], both[64:, TILE:]], axis=0)
 
 
-def forward_attention(q, k, vt, bias, p, att_t):
-    def make_probs(pair):
+def forward_attention(x, w, q, k, v, kt, vt, bias, p, att_t):
+    def make_probs(pair, i):
         cols = pl.ds(pl.multiple_of(pair * 128, 128), 128)
+        span = pl.ds(i * TILE, SPAN)
+        rows = pl.ds(i * TILE, TILE)
+        scores = nt(k[span, cols], two_heads(q[rows, cols])) + bias[i]
+        peak = jnp.max(scores, axis=0, keepdims=True)
+        raised = jnp.exp(scores - peak)
+        total = jnp.sum(raised, axis=0, keepdims=True)
+        p[pair * TILES + i] = (raised * (1.0 / total)).astype(BF16)
+
+    def attend(pair, i):
+        cols = pl.ds(pl.multiple_of(pair * 128, 128), 128)
+        span = pl.ds(i * TILE, SPAN)
+        rows = pl.ds(i * TILE, TILE)
+        att_t[cols, rows] = own_halves(nn(vt[cols, span], p[pair * TILES + i])).astype(BF16)
+
+    def project(n, i):
+        if i == 0:
+            project_queries(n, x, w, q)
+        elif i == 1:
+            project_extended(n, x, w.at[1], k, kt)
+        else:
+            project_extended(n, x, w.at[2], v, vt)
+
+    def make_pair(pair):
         for i in range(TILES):
-            span = pl.ds(i * TILE, SPAN)
-            rows = pl.ds(i * TILE, TILE)
-            scores = nt(k[span, cols], two_heads(q[rows, cols])) + bias[i]
-            peak = jnp.max(scores, axis=0, keepdims=True)
-            raised = jnp.exp(scores - peak)
-            total = jnp.sum(raised, axis=0, keepdims=True)
-            p[pair * TILES + i] = (raised * (1.0 / total)).astype(BF16)
-
-    def attend(pair):
-        cols = pl.ds(pl.multiple_of(pair * 128, 128), 128)
+            make_probs(pair, i)
+
+    def attend_pair(pair):
         for i in range(TILES):
-            span = pl.ds(i * TILE, SPAN)
-            rows = pl.ds(i * TILE, TILE)
-            att_t[cols, rows] = own_halves(nn(vt[cols, span], p[pair * TILES + i])).astype(BF16)
-
-    make_probs(0)
-
-    @pl.loop(1, PAIRS)
-    def _(pair):
-        attend(pair - 1)
-        make_probs(pair)
-
-    attend(PAIRS - 1)
+            attend(pair, i)
+
+    def project_group(n):
+        for i in range(3):
+            project(n, i)
+
+    project_group(0)
+    make_pair(0)
+    project_group(1)
+    attend_pair(0)
+    make_pair(1)
+
+    @pl.loop(1, GROUPS - 1)
+    def _(g):
+        attend_pair(2 * g - 1)
+        make_pair(2 * g)
+        project_group(g + 1)
+        attend_pair(2 * g)
+        make_pair(2 * g + 1)
+
+    for pair in (PAIRS - 2, PAIRS - 1):
+        attend_pair(pair - 1)
+        make_pair(pair)
+    attend_pair(PAIRS - 1)
 
 
 def output_backward(x, att_t, d_out, w, d_proj):
@@ -285,8 +312,8 @@
         return pltpu.make_async_remote_copy(
             src_ref=at_axis(self.sums[stage].at[m], dims, axis, target[axis]),
             dst_ref=self.landed[stage].at[steps - 1, m],
-            send_sem=self.send_sems.at[stage, m, steps - 1],
-            recv_sem=self.recv_sems.at[stage, m, steps - 1],
+            send_sem=self.send_sems.at[stage],
+            recv_sem=self.recv_sems.at[stage],
             device_id=device_of(target),
             device_id_type=MESH,
         )
@@ -311,28 +338,97 @@
         order = ROTATIONS[self.turns[m]]
         axis = order[stage]
         dims = [dim for dim in AXES if dim not in order[:stage]]
-        for steps in (1, 3, 2):
-            self.axis_copy(stage, m, steps).wait_recv()
         total = at_axis(self.sums[stage].at[m], dims, axis, self.at[axis])[...].astype(F32)
         for steps in (1, 2, 3):
             total = total + self.landed[stage][steps - 1, m].astype(F32)
         return total
 
+    def await_axis(self, stage, sems):
+        every = self.landed[stage]
+        pltpu.make_async_copy(every, every, sems.at[stage]).wait()
+
     def next_sum(self, stage):
+        self.await_axis(stage - 1, self.recv_sems)
         for m in range(len(self.turns)):
             self.sums[stage][m] = self.axis_total(stage - 1, m).astype(BF16)
         self.send_axis(stage)
 
     def last_sum(self, put):
+        self.await_axis(2, self.recv_sems)
         for m in range(len(self.turns)):
             put(m, self.axis_total(2, m) * GRAD_SCALE)
 
     def drain(self):
         self.core_copy().wait_send()
         for stage in range(3):
-            for m in range(len(self.turns)):
-                for steps in (1, 2, 3):
-                    self.axis_copy(stage, m, steps).wait_send()
+            self.await_axis(stage, self.send_sems)
+
+
+class PlaneReduction(Reduction):
+    def plane_copies(self, m):
+        order = ROTATIONS[self.turns[m]]
+        first, second = [dim for dim in AXES if dim != order[0]]
+        copies = []
+        for steps in range(1, 16):
+            target = along(along(self.at, first, steps // 4), second, steps % 4)
+            copies.append(
+                pltpu.make_async_remote_copy(
+                    src_ref=self.sums[1].at[m, target[first], target[second]],
+                    dst_ref=self.landed[1].at[steps, m],
+                    send_sem=self.send_sems.at[1],
+                    recv_sem=self.recv_sems.at[1],
+                    device_id=device_of(target),
+                    device_id_type=MESH,
+                )
+            )
+        return copies
+
+    def send_axis(self, stage):
+        if stage == 0:
+            super().send_axis(0)
+            return
+        for m in range(len(self.turns)):
+            for copy in self.plane_copies(m):
+                copy.start()
+
+    def await_plane(self, sems):
+        every = self.landed[1].at[pl.ds(1, 15)]
+        pltpu.make_async_copy(every, every, sems.at[1]).wait()
+
+    def last_sum(self, put):
+        self.await_plane(self.recv_sems)
+        for m in range(len(self.turns)):
+            order = ROTATIONS[self.turns[m]]
+            first, second = [dim for dim in AXES if dim != order[0]]
+            total = self.sums[1][m, self.at[first], self.at[second]].astype(F32)
+            for steps in range(1, 16):
+                total = total + self.landed[1][steps, m].astype(F32)
+            put(m, total * GRAD_SCALE)
+
+    def drain(self):
+        self.core_copy().wait_send()
+        self.await_axis(0, self.send_sems)
+        self.await_plane(self.send_sems)
+
+
+def plane_scratch(n):
+    return [
+        pltpu.VMEM((2, n, 4, 4, 4, 16, 128), BF16),
+        pltpu.VMEM((n, 4, 4, 4, 16, 128), BF16),
+        pltpu.VMEM((n, 4, 4, 16, 128), BF16),
+        pltpu.VMEM((3, n, 4, 4, 16, 128), BF16),
+        pltpu.VMEM((16, n, 16, 128), BF16),
+        pltpu.SemaphoreType.DMA((2,)),
+        pltpu.SemaphoreType.DMA((2,)),
+        pltpu.SemaphoreType.DMA((2,)),
+    ]
+
+
+def plane_of(at, refs, turns):
+    parts, from_core, s1, l0, l1, core_sems, send_sems, recv_sems = refs
+    return PlaneReduction(
+        at, parts, from_core, (s1,), (l0, l1), core_sems, send_sems, recv_sems, turns
+    )
 
 
 def reduction_scratch(lead, n):
@@ -345,8 +441,8 @@
         pltpu.VMEM(lead + (3, n, 4, 16, 128), BF16),
         pltpu.VMEM(lead + (3, n, 16, 128), BF16),
         pltpu.SemaphoreType.DMA(lead + (2,)),
-        pltpu.SemaphoreType.DMA(lead + (3, n, 3)),
-        pltpu.SemaphoreType.DMA(lead + (3, n, 3)),
+        pltpu.SemaphoreType.DMA(lead + (3,)),
+        pltpu.SemaphoreType.DMA(lead + (3,)),
     ]
 
 
@@ -373,10 +469,16 @@
         pl.semaphore_signal(
             barrier, inc=1, device_id=device_of(along(at, "y", steps)), device_id_type=MESH
         )
+        for axis in ("x", "z"):
+            for others in (1, 2, 3):
+                target = along(along(at, "y", steps), axis, others)
+                pl.semaphore_signal(
+                    barrier, inc=1, device_id=device_of(target), device_id_type=MESH
+                )
 
 
 def await_greetings():
-    pl.semaphore_wait(pltpu.get_barrier_semaphore(), SEQ - 1 + 3)
+    pl.semaphore_wait(pltpu.get_barrier_semaphore(), SEQ - 1 + 3 + 18)
 
 
 NEAR_STEPS = (1, -1, 2, -2)
@@ -477,18 +579,20 @@
 
 
 def kernel(
-    phonemes, durations, weights, d_out, coarse_in, fine_in, d_phon, d_weights, *scratch
+    phonemes, durations, weights, d_out, coarse_in, fine_in, out_phon, out_weights, *scratch
 ):
     (
-        w, cotan, coarse, fine, dur_own, dur_all, dur_rows, bounds, near, x, xt, oht, q, k, v, kt, vt,
-        bias, p, att_t, d_proj, dq_t, dk, dv, ds, sums_landed, load_sems, dur_sems, near_sems, sum_sems, *rest
+        d_phon, d_weights, lengths, w, cotan, coarse, fine, dur_own, dur_all, dur_rows, bounds, near, x, xt, oht, q, k, v, kt, vt,
+        bias, p, att_t, d_proj, dq_t, dk, dv, ds, sums_landed, load_sems, dur_sems, near_sems, sum_sems, out_sems, *rest
     ) = scratch
-    out_refs, qkv_refs = rest[: len(rest) // 2], rest[len(rest) // 2 :]
+    out_refs, qkv_refs, last_refs = rest[:10], rest[10:20], rest[20:]
     d_att = cotan
     at = place()
     seq = at["seq"]
 
     greet(at)
+    load_lengths = pltpu.make_async_copy(durations, lengths, load_sems.at[8])
+    load_lengths.start()
     tables = [
         pltpu.make_async_copy(coarse_in, coarse, load_sems.at[5]),
         pltpu.make_async_copy(fine_in, fine, load_sems.at[6]),
@@ -502,7 +606,8 @@
         load.start()
 
     dur_own[...] = jnp.zeros_like(dur_own)
-    dur_own[0:1, 0:P_DEV] = durations[...]
+    load_lengths.wait()
+    dur_own[0:1, 0:P_DEV] = lengths[...]
     dur_all[seq] = dur_own[...]
     near[NEAR:, :] = jnp.zeros((NEAR_PAD - NEAR, D), BF16)
     await_greetings()
@@ -528,16 +633,16 @@
     make_inputs(seq, near, bounds, coarse, fine, x, xt, oht)
     for m in range(3):
         loads[m].wait()
-    make_projections(x, w, q, k, v, kt, vt)
-    forward_attention(q, k, vt, bias, p, att_t)
+    forward_attention(x, w, q, k, v, kt, vt, bias, p, att_t)
     loads[3].wait()
     loads[4].wait()
     output_backward(x, att_t, cotan, w, d_proj)
 
     out_turn = reduction_of(at, out_refs, (0, 1, 2, 0))
     turns = [
-        reduction_of(at, [ref.at[g] for ref in qkv_refs], (0, 1, 2)) for g in range(GROUPS)
+        reduction_of(at, [ref.at[g] for ref in qkv_refs], (0, 1, 2)) for g in range(GROUPS - 1)
     ]
+    turns.append(plane_of(at, last_refs, (0, 1, 2)))
 
     def put_out(m, total):
         cols = m * COLS
@@ -572,7 +677,7 @@
         for m in range(3):
 
             def store(core, y, value):
-                qkv_refs[0][g, core, m, y] = value
+                turns[g].parts[core, m, y] = value
 
             weight_grad(products[m], store)
 
@@ -612,6 +717,13 @@
     turns[2].first_sum()
     turns[0].next_sum(1)
 
+    outputs = [
+        pltpu.make_async_copy(d_phon, out_phon.at[0], out_sems.at[0]),
+        pltpu.make_async_copy(d_weights.at[3], out_weights.at[3], out_sems.at[1]),
+        pltpu.make_async_copy(
+            d_weights.at[pl.ds(0, 3)], out_weights.at[pl.ds(0, 3)], out_sems.at[2]
+        ),
+    ]
     near_sums = near
     low_q, low_k, low_v = [x.at[pl.ds(m * NEAR_PAD, NEAR_PAD)] for m in range(3)]
     phoneme_low(oht, dq_t, dk, dv, low_q, low_k, low_v)
@@ -626,17 +738,19 @@
     turns[3].next_sum(1)
     turns[1].next_sum(2)
     out_turn.last_sum(put_out)
+    outputs[1].start()
     turns[2].next_sum(2)
     turns[0].last_sum(put_of(0))
-    turns[3].next_sum(2)
     turns[1].last_sum(put_of(1))
     turns[2].last_sum(put_of(2))
     total = near_sums[2 * P_DEV : 3 * P_DEV, :].astype(F32)
     for i in range(4):
         sum_copy(at, near_sums, sums_landed, sum_sems, i).wait_recv()
         total = total + sums_landed[i].astype(F32)
-    d_phon[0] = total.astype(BF16)
+    d_phon[...] = total.astype(BF16)
+    outputs[0].start()
     turns[3].last_sum(put_of(3))
+    outputs[2].start()
 
     pltpu.make_async_copy(others, others, dur_sems.at[0]).wait()
     for i in range(4):
@@ -645,13 +759,17 @@
     out_turn.drain()
     for turn in turns:
         turn.drain()
+    for copy in outputs:
+        copy.wait()
 
 
 def on_device(phonemes, durations, weights, d_out):
     coarse, fine = position_tables()
-    vmem = pl.BlockSpec(memory_space=pltpu.VMEM)
     hbm = pl.BlockSpec(memory_space=pl.ANY)
     scratch = [
+        pltpu.VMEM((P_DEV, D), BF16),
+        pltpu.VMEM((4, 8, D), F32),
+        pltpu.VMEM((1, P_DEV), jnp.int32),
         pltpu.VMEM((4, D, D), BF16),
         pltpu.VMEM((F_DEV, D), BF16),
         pltpu.VMEM(coarse.shape, F32),
@@ -678,21 +796,23 @@
         pltpu.VMEM((EXT, D), BF16),
         pltpu.VMEM((2, TILES, SPAN, 2 * TILE), BF16),
         pltpu.VMEM((4, P_DEV, D), BF16),
-        pltpu.SemaphoreType.DMA((8,)),
+        pltpu.SemaphoreType.DMA((9,)),
         pltpu.SemaphoreType.DMA((2,)),
         pltpu.SemaphoreType.DMA((2, 4)),
         pltpu.SemaphoreType.DMA((2, 4)),
+        pltpu.SemaphoreType.DMA((3,)),
     ]
     scratch += reduction_scratch((), 4)
-    scratch += reduction_scratch((GROUPS,), 3)
+    scratch += reduction_scratch((GROUPS - 1,), 3)
+    scratch += plane_scratch(3)
     return pl.pallas_call(
         kernel,
         out_shape=(
             jax.ShapeDtypeStruct((1, P_DEV, D), BF16),
             jax.ShapeDtypeStruct((4, 8, D), F32),
         ),
-        in_specs=[hbm, vmem, hbm, hbm, hbm, hbm],
-        out_specs=(vmem, vmem),
+        in_specs=[hbm] * 6,
+        out_specs=(hbm, hbm),
         scratch_shapes=scratch,
         compiler_params=pltpu.CompilerParams(
             collective_id=0, has_side_effects=True, vmem_limit_bytes=62 * 1024 * 1024

time: 80.1 us -> 77 us (0.961)
  Pallas kernels: 76.2 us -> 73.1 us
    pallas_call x1, Pallas kernels: 76.2 us -> 73.1 us  [on_device(): pl.pallas_call(kernel, out_shape=(jax.ShapeDtypeStruct((1, P_DEV, D), BF1...]
where the time goes in v3:
time: 77 us; the launch traced here: 76.9 us
  Pallas kernels  73.1 us (95%)
  local copies, waits for them, and re-layouts  3.11 us (4%)
    pallas_call x1, Pallas kernels, on_device(): pl.pallas_call(kernel, out_shape=(jax.ShapeDtypeStruct((1, P_DEV, D), BF1...  73.1 us
    unnamed x2, local copies, waits for them, and re-layouts  3.11 us

profile of v3, /device:TPU:1, one launch (start us, length us, event | category | flops | bytes accessed | tf_op | source)
XLA Modules:
  0.0 76.9 jit_solution(8279220806940241480)
XLA Ops:
  0.6 73.1 %shard_map.77 = (bf16[1,48,1024]{2,1,0:T(8,128)(2,1)}, f32[4,8,1024]{2,1,0:T(8,128)}) custom-call(bf16[1,48,1024]{2,1,0:T(8,128)(2,1)} %phonemes.1, s32[1,48]{1,0:T(1,128)} %durations.1, bf16[4,1024,1024]{2,1,0:T(8,128)(2,1)} %weights.1, bf16[1,384,1024]{2,1,0:T(8,128)(2,1)} %d_out.1, f32[104,1024]{1,0:T(8,128)} %constant.4.clone.coarse_in, ...), custom_call_target="tpu_custom_call" | custom-call | tf_op jit(solution)/shard_map/pallas_call | solution.py:808
  73.8 1.5 %copy.10 = bf16[1,48,1024]{2,1,0:T(8,128)(2,1)} copy(bf16[1,48,1024]{2,1,0:T(8,128)(2,1)} %get-tuple-element.4) | data formatting | bytes 196608
  75.3 1.6 %copy.11 = f32[4,8,1024]{2,1,0:T(8,128)} copy(f32[4,8,1024]{2,1,0:T(8,128)} %get-tuple-element.5) | data formatting | bytes 262144

commit v4 on v3

--- a/solution.py
+++ b/solution.py
@@ -292,12 +292,12 @@
         self.core_sems, self.send_sems, self.recv_sems = core_sems, send_sems, recv_sems
         self.turns = turns
 
-    def core_copy(self):
+    def core_copy(self, m):
         sibling = dict(self.at)
         sibling["core"] = 1 - self.at["core"]
         return pltpu.make_async_remote_copy(
-            src_ref=self.parts.at[sibling["core"]],
-            dst_ref=self.from_core,
+            src_ref=self.parts.at[sibling["core"], m],
+            dst_ref=self.from_core.at[m],
             send_sem=self.core_sems.at[0],
             recv_sem=self.core_sems.at[1],
             device_id=device_of(sibling),
@@ -318,8 +318,11 @@
             device_id_type=MESH,
         )
 
-    def send_core(self):
-        self.core_copy().start()
+    def send_core(self, m):
+        self.core_copy(m).start()
+
+    def await_core(self, side):
+        pltpu.make_async_copy(self.from_core, self.from_core, self.core_sems.at[side]).wait()
 
     def send_axis(self, stage):
         for m in range(len(self.turns)):
@@ -327,11 +330,10 @@
                 self.axis_copy(stage, m, steps).start()
 
     def first_sum(self):
-        self.core_copy().wait_recv()
+        self.await_core(1)
         for m in range(len(self.turns)):
             for y in range(4):
-                total = self.sums[0][m, y].astype(F32) + self.from_core[m, y].astype(F32)
-                self.sums[0][m, y] = total.astype(BF16)
+                self.sums[0][m, y] = self.sums[0][m, y] + self.from_core[m, y]
         self.send_axis(0)
 
     def axis_total(self, stage, m):
@@ -359,7 +361,7 @@
             put(m, self.axis_total(2, m) * GRAD_SCALE)
 
     def drain(self):
-        self.core_copy().wait_send()
+        self.await_core(0)
         for stage in range(3):
             self.await_axis(stage, self.send_sems)
 
@@ -406,7 +408,7 @@
             put(m, total * GRAD_SCALE)
 
     def drain(self):
-        self.core_copy().wait_send()
+        self.await_core(0)
         self.await_axis(0, self.send_sems)
         self.await_plane(self.send_sems)
 
@@ -665,6 +667,7 @@
                 out_refs[0][core, j, y] = value
 
             weight_grad(lambda rows: nn(att_t[rows, :], d_proj[:, cols]), store)
+            out_turn.send_core(j)
 
     def group_grads(g):
         cols = pl.ds(g * COLS, COLS)
@@ -680,6 +683,7 @@
                 turns[g].parts[core, m, y] = value
 
             weight_grad(products[m], store)
+            turns[g].send_core(m)
 
     def both_phases(pair):
         if pair + 1 < PAIRS:
@@ -687,34 +691,29 @@
         pair_grads(pair, q, kt, d_att, p, ds, dq_t, dk, dv)
 
     out_grads()
-    out_turn.send_core()
     attended_grads(w, d_proj, d_att)
 
     score_grads(0, v, d_att, p, ds)
     both_phases(0)
     both_phases(1)
     group_grads(0)
-    turns[0].send_core()
     out_turn.first_sum()
 
     both_phases(2)
     both_phases(3)
     group_grads(1)
-    turns[1].send_core()
     turns[0].first_sum()
 
     both_phases(4)
     both_phases(5)
     group_grads(2)
-    turns[2].send_core()
     turns[1].first_sum()
     out_turn.next_sum(1)
 
     both_phases(6)
+    turns[2].first_sum()
     both_phases(7)
     group_grads(3)
-    turns[3].send_core()
-    turns[2].first_sum()
     turns[0].next_sum(1)
 
     outputs = [
@@ -726,20 +725,20 @@
     ]
     near_sums = near
     low_q, low_k, low_v = [x.at[pl.ds(m * NEAR_PAD, NEAR_PAD)] for m in range(3)]
+    turns[3].first_sum()
+    out_turn.next_sum(2)
+    turns[1].next_sum(1)
     phoneme_low(oht, dq_t, dk, dv, low_q, low_k, low_v)
-    turns[3].first_sum()
-    turns[1].next_sum(1)
-    out_turn.next_sum(2)
+    turns[2].next_sum(1)
     phoneme_sums(oht, d_proj, w, low_q, low_k, low_v, near_sums)
     for i in range(4):
         sum_copy(at, near_sums, sums_landed, sum_sems, i).start()
-    turns[2].next_sum(1)
+    turns[3].next_sum(1)
     turns[0].next_sum(2)
-    turns[3].next_sum(1)
     turns[1].next_sum(2)
+    turns[2].next_sum(2)
     out_turn.last_sum(put_out)
     outputs[1].start()
-    turns[2].next_sum(2)
     turns[0].last_sum(put_of(0))
     turns[1].last_sum(put_of(1))
     turns[2].last_sum(put_of(2))

time: 77 us -> 77.4 us (level)
  no operation moved by 1% of the time
where the time goes in v4:
time: 77.4 us; the launch traced here: 77.2 us
  Pallas kernels  73.5 us (95%)
  local copies, waits for them, and re-layouts  3.11 us (4%)
    pallas_call x1, Pallas kernels, on_device(): pl.pallas_call(kernel, out_shape=(jax.ShapeDtypeStruct((1, P_DEV, D), BF1...  73.5 us
    unnamed x2, local copies, waits for them, and re-layouts  3.11 us

profile of v4, /device:TPU:1, one launch (start us, length us, event | category | flops | bytes accessed | tf_op | source)
XLA Modules:
  0.0 77.2 jit_solution(15405838764938449174)
XLA Ops:
  0.6 73.5 %shard_map.77 = (bf16[1,48,1024]{2,1,0:T(8,128)(2,1)}, f32[4,8,1024]{2,1,0:T(8,128)}) custom-call(bf16[1,48,1024]{2,1,0:T(8,128)(2,1)} %phonemes.1, s32[1,48]{1,0:T(1,128)} %durations.1, bf16[4,1024,1024]{2,1,0:T(8,128)(2,1)} %weights.1, bf16[1,384,1024]{2,1,0:T(8,128)(2,1)} %d_out.1, f32[104,1024]{1,0:T(8,128)} %constant.4.clone.coarse_in, ...), custom_call_target="tpu_custom_call" | custom-call | tf_op jit(solution)/shard_map/pallas_call | solution.py:807
  74.1 1.5 %copy.10 = bf16[1,48,1024]{2,1,0:T(8,128)(2,1)} copy(bf16[1,48,1024]{2,1,0:T(8,128)(2,1)} %get-tuple-element.4) | data formatting | bytes 196608
  75.6 1.6 %copy.11 = f32[4,8,1024]{2,1,0:T(8,128)} copy(f32[4,8,1024]{2,1,0:T(8,128)} %get-tuple-element.5) | data formatting | bytes 262144
